TPU v7x, 32 devices: a whole 2x2x4 slice. The times are simulated.
32 devices in a mesh: tm: 4 (over y, x), space: 8 (over z, core).
Axes of the slice: x: 2, y: 2, z: 4, core: 2. Of those that a mesh axis runs over, the one named last changes fastest.
Arguments:
- latent_clip: bfloat16 [8, 16, 32, 256], P('tm', 'space'), may hold values from -45 to 45
- cotangent: bfloat16 [8, 16, 32, 128], P('tm', 'space'), may hold values from -6 to 6
- conv_weight: bfloat16 [6912, 128], replicated, may hold values from -0.078125 to 0.078125
- norm_gain: float32 [256], replicated, may hold values from 0.5 to 1.5
- norm_shift: float32 [256], replicated, may hold values from -2 to 2
Outputs:
- clip_grad: bfloat16 [8, 16, 32, 256], P('tm', 'space')
- weight_grad: float32 [6912, 128], P('space')
- gain_grad: float32 [256], replicated
- shift_grad: float32 [256], replicated
All inputs are finite; a program needn't handle non-finite values.
Results may differ from a plain program's by a relative error of at most 0.0029.
Values may be sent and summed in bfloat16 or wider, within the bound.
A program may use at most 64 MiB of HBM per device.

v0:
```python
import jax
import jax.numpy as jnp
from jax import lax
from jax.sharding import PartitionSpec as P

GROUPS = 32


def shifted(value, axis, steps):
    count = lax.axis_size(axis)
    leading, last = (max(0, -steps), min(count, count - steps))
    return lax.ppermute(value, axis, [(source, source + steps) for source in range(leading, last)])


def extended_2(block, sides, width):
    for axis, dim in sides:
        count = lax.axis_size(axis)
        forward = [(i, i + 1) for i in range(count - 1)]
        backward = [(target, source) for source, target in forward]
        low = lax.ppermute(
            lax.slice_in_dim(block, block.shape[dim] - width, None, axis=dim), axis, forward
        )
        high = lax.ppermute(lax.slice_in_dim(block, 0, width, axis=dim), axis, backward)
        block = jnp.concatenate([low, block, high], axis=dim)
    return block


def silu_slope(activation):
    sigma = jax.nn.sigmoid(activation)
    return sigma * (1.0 + activation * (1.0 - sigma))


def tap_block(source, anchors, frame_count, row_count, col_count):
    pieces = [
        source[
            anchor[0] : anchor[0] + frame_count,
            anchor[1] : anchor[1] + row_count,
            anchor[2] : anchor[2] + col_count,
            :,
        ]
        for anchor in anchors
    ]
    merged = jnp.concatenate(pieces, axis=-1)
    return merged.reshape(frame_count * row_count * col_count, merged.shape[-1])


def transposed(grad_pad, conv_weight, frame_count, row_count, col_count):
    out_channels = conv_weight.shape[1]
    channels = conv_weight.shape[0] // 27
    kernel = conv_weight.reshape(3, 3, 3, channels, out_channels)
    total = jnp.zeros((frame_count * row_count * col_count, channels), jnp.float32)
    for tap_time in range(3):
        anchors = [
            (2 - tap_time, 2 - tap_row, 2 - tap_col) for tap_row in range(3) for tap_col in range(3)
        ]
        tap_cols = tap_block(grad_pad, anchors, frame_count, row_count, col_count)
        flipped = jnp.transpose(kernel[tap_time], (0, 1, 3, 2)).reshape(9 * out_channels, channels)
        total = total + jnp.dot(tap_cols, flipped, preferred_element_type=jnp.float32)
    return total.reshape(frame_count, row_count, col_count, channels)


def shards(latent_clip, cotangent, conv_weight, norm_gain, norm_shift):
    frame_count, row_count, col_count, channels = latent_clip.shape
    out_channels = cotangent.shape[-1]
    width_group = channels // GROUPS
    tm_size = lax.axis_size("tm")
    space_size = lax.axis_size("space")
    group_count = frame_count * row_count * col_count * width_group * tm_size * space_size
    values = latent_clip.astype(jnp.float32).reshape(
        frame_count, row_count, col_count, GROUPS, width_group
    )
    group_mean = lax.psum(jnp.sum(values, axis=(0, 1, 2, 4)), ("tm", "space")) / group_count
    centered = values - group_mean[:, None]
    group_var = (
        lax.psum(jnp.sum(centered * centered, axis=(0, 1, 2, 4)), ("tm", "space")) / group_count
    )
    inv_std = lax.rsqrt(group_var + 1e-06)
    normed = (centered * inv_std[:, None]).reshape(frame_count, row_count, col_count, channels)
    activation = normed * norm_gain + norm_shift
    hidden = jax.nn.silu(activation).astype(jnp.bfloat16)
    ahead = shifted(cotangent, "tm", -1)
    time_source = jnp.concatenate([cotangent, ahead], axis=0)
    time_pad = (0, 0)
    cached = shifted(hidden, "tm", 1)
    extended = jnp.concatenate([cached, hidden], axis=0)
    rimmed = extended_2(extended, (("space", 1),), 1)
    padded = jnp.pad(rimmed, ((0, 0), (0, 0), (1, 1), (0, 0)))
    cell_count = frame_count * row_count * col_count
    upstream = cotangent.reshape(cell_count, out_channels)
    tap_grads = []
    for tap_time in range(3):
        anchors = [(tap_time, tap_row, tap_col) for tap_row in range(3) for tap_col in range(3)]
        tap_cols = tap_block(padded, anchors, frame_count, row_count, col_count)
        tap_grads.append(
            lax.dot_general(
                tap_cols, upstream, (((0,), (0,)), ((), ())), preferred_element_type=jnp.float32
            )
        )
    local_grad = jnp.concatenate(tap_grads, axis=0)
    space_shard = lax.psum_scatter(local_grad, "space", scatter_dimension=0, tiled=True)
    weight_grad = lax.psum(space_shard, "tm")
    grad_pad = jnp.pad(time_source, (time_pad, (2, 2), (1, 1), (0, 0)))
    spread = transposed(grad_pad, conv_weight, frame_count, row_count + 2, col_count)
    from_below = shifted(spread[:, 0], "space", -1)
    from_above = shifted(spread[:, row_count + 1], "space", 1)
    inner = spread[:, 1 : row_count + 1]
    inner = inner.at[:, row_count - 1].add(from_below)
    inner = inner.at[:, 0].add(from_above)
    activation_grad = inner * silu_slope(activation)
    gain_grad, shift_grad = lax.psum(
        (
            jnp.sum(activation_grad * normed, axis=(0, 1, 2)),
            jnp.sum(activation_grad, axis=(0, 1, 2)),
        ),
        ("tm", "space"),
    )
    first = jnp.sum((norm_gain * shift_grad).reshape(GROUPS, width_group), axis=1)
    second = jnp.sum((norm_gain * gain_grad).reshape(GROUPS, width_group), axis=1)
    scaled = (activation_grad * norm_gain).reshape(
        frame_count, row_count, col_count, GROUPS, width_group
    )
    normed_groups = normed.reshape(frame_count, row_count, col_count, GROUPS, width_group)
    clip_grad = inv_std[:, None] * (
        scaled - first[:, None] / group_count - normed_groups * second[:, None] / group_count
    )
    clip_grad = clip_grad.reshape(frame_count, row_count, col_count, channels).astype(jnp.bfloat16)
    return (clip_grad, weight_grad, gain_grad, shift_grad)


def solution(mesh):
    return jax.shard_map(
        shards,
        mesh=mesh,
        in_specs=(P("tm", "space", None, None), P("tm", "space", None, None), P(), P(), P()),
        out_specs=(P("tm", "space", None, None), P("space", None), P(), P()),
        check_vma=False,
    )
```

profile of v0, /device:TPU:0, one launch (start us, length us, event | category | flops | bytes accessed | tf_op | source)
XLA Modules:
  0.0 225.5 jit_solution(13261450040164895884)
XLA Ops:
  7.2 0.9 convert_reduce_fusion
  8.1 0.1 reduce_sum.69
  8.2 0.1 reduce_sum.70
  8.3 1.3 collective-permute-start
  9.6 43.2 %psum.35 = f32[32]{0:T(128)S(1)} all-reduce(f32[32]{0:T(128)S(1)} %reduce_sum.70), channel_id=1, replica_groups=mesh['tm'=4,'space'=8] {'tm','space'}, use_global_device_ids=true, to_apply=%region_2.0 | all-reduce | flops 32 | bytes 256 | tf_op jit(solution)/shard_map/psum | solution.py:72
  52.8 0.1 sub.35
  52.8 0.1 sub.36
  52.9 0.9 fusion.33
  53.8 0.1 reduce_sum.72
  53.9 0.1 reduce_sum.73
  54.0 1.5 fusion.40
  55.6 41.0 %psum.36 = f32[32]{0:T(128)S(1)} all-reduce(f32[32]{0:T(128)S(1)} %reduce_sum.73), channel_id=1, replica_groups=mesh['tm'=4,'space'=8] {'tm','space'}, use_global_device_ids=true, to_apply=%region_5.6 | all-reduce | flops 32 | bytes 256 | tf_op jit(solution)/shard_map/psum | solution.py:75
  96.6 0.2 copy.15
  96.8 0.2 copy.13
  97.1 0.2 copy.14
  97.3 0.2 copy-done.1
  97.8 0.1 constant_dynamic-update-slice_fusion.23
  98.0 0.1 constant_dynamic-update-slice_fusion.20
  98.1 0.1 constant_dynamic-update-slice_fusion.19
  98.3 0.3 fusion.42
  98.6 0.3 convolution_add_fusion.1
  99.0 0.3 convolution_add_fusion
  99.4 1.3 collective-permute-start.1
  100.8 0.1 mul.76
  100.9 3.0 %collective-permute-start.2 = (f32[2,32,256]{2,1,0:T(8,128)S(1)}, f32[2,32,256]{2,1,0:T(8,128)S(1)}, u32[]{:S(2)}, u32[]{:S(2)}) collective-permute-start(f32[2,32,256]{2,1,0:T(8,128)S(1)} %get-tuple-element.53), channel_id=1, source_target_pairs={{0,1},{1,2},{2,3},{3,4},{4,5},{5,6},{6,7},{8,9},{9,10},{10,11},{11... | collective-permute-start | bytes 196616 | tf_op jit(solution)/shard_map/ppermute | solution.py:12
  103.9 0.9 collective-permute-done.2
  104.8 0.1 fusion.38
  105.0 4.2 %collective-permute-start.3 = (bf16[2,2,32,256]{3,2,1,0:T(8,128)(2,1)S(1)}, bf16[2,2,32,256]{3,2,1,0:T(8,128)(2,1)S(1)}, u32[]{:S(2)}, u32[]{:S(2)}) collective-permute-start(bf16[2,2,32,256]{3,2,1,0:T(8,128)(2,1)S(1)} %get-tuple-element.90), channel_id=1, source_target_pairs={{0,8},{8,16},{16,24},{1,9},{9,17},{17,25},{2,10},{10,18},{18,26},{... | collective-permute-start | bytes 196616 | tf_op jit(solution)/shard_map/ppermute | solution.py:12
  109.1 1.9 collective-permute-done.3
  111.1 1.4 collective-permute-start.4
  112.6 1.3 collective-permute-start.5
  113.9 4.6 %collective-permute-done.5 = bf16[4,1,32,256]{3,2,1,0:T(8,128)(2,1)S(1)} collective-permute-done((bf16[4,1,32,256]{3,2,1,0:T(8,128)(2,1)S(1)}, bf16[4,1,32,256]{3,2,1,0:T(8,128)(2,1)S(1)}, u32[]{:S(2)}, u32[]{:S(2)}) %collective-permute-start.5) | collective-permute-done | bytes 65568 | tf_op jit(solution)/shard_map/ppermute | solution.py:23
  118.4 0.1 select_maximum_fusion
  118.9 0.3 convolution_bitcast_fusion
  119.2 0.3 convolution_bitcast_fusion.2
  119.6 0.3 convolution_bitcast_fusion.1
  119.9 2.0 pad_maximum_fusion
  122.0 45.1 %all-reduce.2 = (f32[256]{0:T(256)S(1)}, f32[256]{0:T(256)S(1)}) all-reduce(f32[256]{0:T(256)S(1)} %get-tuple-element.29, f32[256]{0:T(256)S(1)} %get-tuple-element.28), channel_id=1, replica_groups=mesh['tm'=4,'space'=8] {'tm','space'}, use_global_device_ids=true, to_apply=%region_10.11 | all-reduce | flops 512 | bytes 4096 | tf_op jit(solution)/shard_map/psum | solution.py:110
  167.2 0.1 reshape.151
  167.2 0.1 reduce_sum.75
  167.4 3.1 %reduce-scatter.2.cloned.1.call-done = f32[864,128]{1,0:T(8,128)} async-done(((f32[6912,128]{1,0:T(8,128)}), f32[864,128]{1,0:T(8,128)}) %reduce-scatter.2.cloned.1.call-update) | async-done | bytes 442384 | tf_op jit(solution)/shard_map/reduce_scatter | solution.py:100
  170.6 0.1 sub.41
  170.7 0.1 reshape.152
  170.8 0.1 reduce_sum.77
  171.0 0.1 mul.89
  171.1 0.7 fusion.32
  171.8 45.1 %all-reduce.5.cloned.1.call-done = f32[864,128]{1,0:T(8,128)} async-done(((f32[864,128]{1,0:T(8,128)}), f32[864,128]{1,0:T(8,128)}) %all-reduce.5.cloned.1.call-update) | async-done | bytes 442384 | tf_op jit(solution)/shard_map/psum | solution.py:101
  216.9 1.8 copy.74
  (51 shorter events, 1.1 us)
Async XLA Ops:
  7.2 163.3 %reduce-scatter.2.cloned.1.call-start = ((), (), s32[]{:S(2)}) async-start(), calls=%async_computation.1 | async-start | bytes 3981312 | tf_op jit(solution)/shard_map/reduce_scatter | solution.py:100
  8.3 89.0 %collective-permute-start = (bf16[2,2,32,128]{3,2,1,0:T(8,128)(2,1)}, bf16[2,2,32,128]{3,2,1,0:T(8,128)(2,1)S(1)}, u32[]{:S(2)}, u32[]{:S(2)}) collective-permute-start(bf16[2,2,32,128]{3,2,1,0:T(8,128)(2,1)} %param.10), channel_id=1, source_target_pairs={{8,0},{16,8},{24,16},{9,1},{17,9},{25,17},{10,2},{18,10},{26,18},{... | collective-permute-start | bytes 98312 | tf_op jit(solution)/shard_map/ppermute | solution.py:12
  96.8 0.8 copy-start.1
  99.0 5.8 %copy-start = (bf16[2,2,32,256]{3,2,1,0:T(8,128)(2,1)S(1)}, bf16[2,2,32,256]{3,2,1,0:T(8,128)(2,1)}, u32[]{:S(2)}) copy-start(bf16[2,2,32,256]{3,2,1,0:T(8,128)(2,1)} %param.9) | copy-start | bytes 196612
  99.0 5.8 %copy-start.2 = (f32[256]{0:T(256)S(1)}, f32[256]{0:T(256)}, u32[]{:S(2)}) copy-start(f32[256]{0:T(256)} %param.12) | copy-start | bytes 3076
  99.0 5.8 %copy-start.3 = (f32[256]{0:T(256)S(1)}, f32[256]{0:T(256)}, u32[]{:S(2)}) copy-start(f32[256]{0:T(256)} %param.13) | copy-start | bytes 3076
  99.4 4.5 %collective-permute-start.1 = (f32[2,32,256]{2,1,0:T(8,128)S(1)}, f32[2,32,256]{2,1,0:T(8,128)S(1)}, u32[]{:S(2)}, u32[]{:S(2)}) collective-permute-start(f32[2,32,256]{2,1,0:T(8,128)S(1)} %get-tuple-element.54), channel_id=1, source_target_pairs={{1,0},{2,1},{3,2},{4,3},{5,4},{6,5},{7,6},{9,8},{10,9},{11,10},{12... | collective-permute-start | bytes 196616 | tf_op jit(solution)/shard_map/ppermute | solution.py:12
  100.9 3.9 %collective-permute-start.2 = (f32[2,32,256]{2,1,0:T(8,128)S(1)}, f32[2,32,256]{2,1,0:T(8,128)S(1)}, u32[]{:S(2)}, u32[]{:S(2)}) collective-permute-start(f32[2,32,256]{2,1,0:T(8,128)S(1)} %get-tuple-element.53), channel_id=1, source_target_pairs={{0,1},{1,2},{2,3},{3,4},{4,5},{5,6},{6,7},{8,9},{9,10},{10,11},{11... | collective-permute-start | bytes 196616 | tf_op jit(solution)/shard_map/ppermute | solution.py:12
  105.0 6.1 %collective-permute-start.3 = (bf16[2,2,32,256]{3,2,1,0:T(8,128)(2,1)S(1)}, bf16[2,2,32,256]{3,2,1,0:T(8,128)(2,1)S(1)}, u32[]{:S(2)}, u32[]{:S(2)}) collective-permute-start(bf16[2,2,32,256]{3,2,1,0:T(8,128)(2,1)S(1)} %get-tuple-element.90), channel_id=1, source_target_pairs={{0,8},{8,16},{16,24},{1,9},{9,17},{17,25},{2,10},{10,18},{18,26},{... | collective-permute-start | bytes 196616 | tf_op jit(solution)/shard_map/ppermute | solution.py:12
  111.1 2.8 %collective-permute-start.4 = (bf16[4,1,32,256]{3,2,1,0:T(8,128)(2,1)S(1)}, bf16[4,1,32,256]{3,2,1,0:T(8,128)(2,1)S(1)}, u32[]{:S(2)}, u32[]{:S(2)}) collective-permute-start(bf16[4,1,32,256]{3,2,1,0:T(8,128)(2,1)S(1)} %get-tuple-element.88), channel_id=1, source_target_pairs={{0,1},{1,2},{2,3},{3,4},{4,5},{5,6},{6,7},{8,9},{9,10},{10,11},{11... | collective-permute-start | bytes 196616 | tf_op jit(solution)/shard_map/ppermute | solution.py:20
  112.6 5.9 %collective-permute-start.5 = (bf16[4,1,32,256]{3,2,1,0:T(8,128)(2,1)S(1)}, bf16[4,1,32,256]{3,2,1,0:T(8,128)(2,1)S(1)}, u32[]{:S(2)}, u32[]{:S(2)}) collective-permute-start(bf16[4,1,32,256]{3,2,1,0:T(8,128)(2,1)S(1)} %get-tuple-element.89), channel_id=1, source_target_pairs={{1,0},{2,1},{3,2},{4,3},{5,4},{6,5},{7,6},{9,8},{10,9},{11,10},{12... | collective-permute-start | bytes 196616 | tf_op jit(solution)/shard_map/ppermute | solution.py:23
  122.0 94.9 %all-reduce.5.cloned.1.call-start = ((), (), s32[]{:S(2)}) async-start(), calls=%async_computation.2 | async-start | bytes 884736 | tf_op jit(solution)/shard_map/psum | solution.py:101
  167.2 51.5 %copy-start.4 = (f32[256]{0:T(256)}, f32[256]{0:T(256)S(1)}, u32[]{:S(2)}) copy-start(f32[256]{0:T(256)S(1)} %get-tuple-element.97) | copy-start | bytes 3076
  167.2 51.5 %copy-start.5 = (f32[256]{0:T(256)}, f32[256]{0:T(256)S(1)}, u32[]{:S(2)}) copy-start(f32[256]{0:T(256)S(1)} %get-tuple-element.98) | copy-start | bytes 3076
Sparse Core Ops, SparseCore 0:
  122.1 48.3 reduce-scatter.1
  173.8 43.0 all-reduce.4
where the time goes:
time: 226 us
  blocking collectives  129 us (57%)
  waiting for transfers between devices  55.6 us (25%)
  between operations  14.5 us (6%)
  starting transfers between devices  12.6 us (6%)
  local copies, waits for them, and re-layouts  6.15 us (3%)
  other arithmetic  5.25 us (2%)
    psum x1, blocking collectives, shards(): lax.psum((jnp.sum(activation_grad * normed, axis=(0, 1, 2)), jnp.sum(acti...  45.1 us
    psum x1, waiting for transfers between devices, shards(): weight_grad = lax.psum(space_shard, 'tm')  45.1 us
    psum x1, blocking collectives, shards(): lax.psum(jnp.sum(values, axis=(0, 1, 2, 4)), ('tm', 'space')) / group_count  43.2 us
    psum x1, blocking collectives, shards(): lax.psum(jnp.sum(centered * centered, axis=(0, 1, 2, 4)), ('tm', 'space'))  41 us
    ppermute x4, starting transfers between devices, shifted(): lax.ppermute(value, axis, [(source, source + steps) for source in range(l...  9.8 us
    ppermute x1, waiting for transfers between devices, extended_2(): lax.ppermute(lax.slice_in_dim(block, 0, width, axis=dim), axis, backward)  4.55 us
  transfers between devices with their start and end apart: 8, of which 5 were waited for; matrix products, arithmetic and copies ran while one was open for 2% of the time, Pallas kernels for 0%

commit v1 on v0

--- a/solution.py
+++ b/solution.py
@@ -1,9 +1,20 @@
+import functools
 import jax
 import jax.numpy as jnp
 from jax import lax
 from jax.sharding import PartitionSpec as P
+from jax.lax import all_gather
 
 GROUPS = 32
+
+
+def draft_point(unit, across):
+    opened = all_gather(unit, across)
+    mid_arr = jnp.sum(opened, 0)
+    return mid_arr
+
+
+counts_answer = functools.partial(draft_point, across="tm")
 
 
 def shifted(value, axis, steps):
@@ -98,7 +109,7 @@
         )
     local_grad = jnp.concatenate(tap_grads, axis=0)
     space_shard = lax.psum_scatter(local_grad, "space", scatter_dimension=0, tiled=True)
-    weight_grad = lax.psum(space_shard, "tm")
+    weight_grad = counts_answer(space_shard)
     grad_pad = jnp.pad(time_source, (time_pad, (2, 2), (1, 1), (0, 0)))
     spread = transposed(grad_pad, conv_weight, frame_count, row_count + 2, col_count)
     from_below = shifted(spread[:, 0], "space", -1)

time: 226 us -> 219 us (0.969)
  blocking collectives: 129 us -> 122 us
  other arithmetic: 5.25 us -> 7.62 us
    psum x1 -> x0, waiting for transfers between devices: 45.1 us -> none  [shards(): weight_grad = lax.psum(space_shard, 'tm')]
    reduce_scatter x1, waiting for transfers between devices: 3.13 us -> 47.5 us  [shards(): lax.psum_scatter(local_grad, 'space', scatter_dimension=0, tiled=True)]
    psum x1, blocking collectives: 45.1 us -> 38.1 us  [shards(): lax.psum((jnp.sum(activation_grad * normed, axis=(0, 1, 2)), jnp.sum(acti...]
    reduce_sum x0 -> x1, other arithmetic: none -> 2.38 us  [draft_point(): mid_arr = jnp.sum(opened, 0)]
  transfers between devices with their start and end apart: 8 -> 8, of which waited for: 5 -> 4; matrix products, arithmetic and copies ran while one was open for 2% -> 2% of each run, Pallas kernels for 0% -> 0%
where the time goes in v1:
time: 219 us; the launch traced here: 218 us
  blocking collectives  122 us (56%)
  waiting for transfers between devices  54.8 us (25%)
  between operations  14.5 us (7%)
  starting transfers between devices  12.6 us (6%)
  other arithmetic  7.62 us (3%)
  local copies, waits for them, and re-layouts  4.12 us (2%)
    reduce_scatter x1, waiting for transfers between devices, shards(): lax.psum_scatter(local_grad, 'space', scatter_dimension=0, tiled=True)  47.5 us
    psum x1, blocking collectives, shards(): lax.psum(jnp.sum(values, axis=(0, 1, 2, 4)), ('tm', 'space')) / group_count  43.2 us
    psum x1, blocking collectives, shards(): lax.psum(jnp.sum(centered * centered, axis=(0, 1, 2, 4)), ('tm', 'space'))  41 us
    psum x1, blocking collectives, shards(): lax.psum((jnp.sum(activation_grad * normed, axis=(0, 1, 2)), jnp.sum(acti...  38.1 us
    ppermute x4, starting transfers between devices, shifted(): lax.ppermute(value, axis, [(source, source + steps) for source in range(l...  9.8 us
    ppermute x1, waiting for transfers between devices, extended_2(): lax.ppermute(lax.slice_in_dim(block, 0, width, axis=dim), axis, backward)  4.55 us
  transfers between devices with their start and end apart: 8, of which 4 were waited for; matrix products, arithmetic and copies ran while one was open for 2% of the time, Pallas kernels for 0%

profile of v1, /device:TPU:0, one launch (start us, length us, event | category | flops | bytes accessed | tf_op | source)
XLA Modules:
  0.0 218.0 jit_solution(15247144118623093506)
XLA Ops:
  7.2 0.9 convert_reduce_fusion
  8.1 0.1 reduce_sum.78
  8.2 0.1 reduce_sum.79
  8.3 1.3 collective-permute-start
  9.6 43.2 %psum.28 = f32[32]{0:T(128)S(1)} all-reduce(f32[32]{0:T(128)S(1)} %reduce_sum.79), channel_id=1, replica_groups=mesh['tm'=4,'space'=8] {'tm','space'}, use_global_device_ids=true, to_apply=%region_2.0 | all-reduce | flops 32 | bytes 256 | tf_op jit(solution)/shard_map/psum | solution.py:83
  52.8 0.1 sub.35
  52.8 0.1 sub.36
  52.9 0.9 fusion.33
  53.8 0.1 reduce_sum.81
  53.9 0.1 reduce_sum.82
  54.0 1.5 fusion.40
  55.6 41.0 %psum.29 = f32[32]{0:T(128)S(1)} all-reduce(f32[32]{0:T(128)S(1)} %reduce_sum.82), channel_id=1, replica_groups=mesh['tm'=4,'space'=8] {'tm','space'}, use_global_device_ids=true, to_apply=%region_5.6 | all-reduce | flops 32 | bytes 256 | tf_op jit(solution)/shard_map/psum | solution.py:86
  96.6 0.2 copy.15
  96.8 0.2 copy.13
  97.1 0.2 copy.14
  97.4 0.1 constant_dynamic-update-slice_fusion.25
  97.6 0.1 constant_dynamic-update-slice_fusion.23
  97.7 0.1 constant_dynamic-update-slice_fusion.22
  97.8 0.1 constant_dynamic-update-slice_fusion.20
  97.9 0.1 constant_dynamic-update-slice_fusion.19
  98.0 0.3 fusion.42
  98.4 0.3 convolution_add_fusion.1
  98.8 0.3 convolution_add_fusion
  99.2 1.3 collective-permute-start.1
  100.5 0.1 mul.76
  100.6 3.0 %collective-permute-start.2 = (f32[2,32,256]{2,1,0:T(8,128)S(1)}, f32[2,32,256]{2,1,0:T(8,128)S(1)}, u32[]{:S(2)}, u32[]{:S(2)}) collective-permute-start(f32[2,32,256]{2,1,0:T(8,128)S(1)} %get-tuple-element.53), channel_id=1, source_target_pairs={{0,1},{1,2},{2,3},{3,4},{4,5},{5,6},{6,7},{8,9},{9,10},{10,11},{11... | collective-permute-start | bytes 196616 | tf_op jit(solution)/shard_map/ppermute | solution.py:23
  103.7 0.9 collective-permute-done.2
  104.6 0.1 fusion.38
  104.7 4.2 %collective-permute-start.3 = (bf16[2,2,32,256]{3,2,1,0:T(8,128)(2,1)S(1)}, bf16[2,2,32,256]{3,2,1,0:T(8,128)(2,1)S(1)}, u32[]{:S(2)}, u32[]{:S(2)}) collective-permute-start(bf16[2,2,32,256]{3,2,1,0:T(8,128)(2,1)S(1)} %get-tuple-element.90), channel_id=1, source_target_pairs={{0,8},{8,16},{16,24},{1,9},{9,17},{17,25},{2,10},{10,18},{18,26},{... | collective-permute-start | bytes 196616 | tf_op jit(solution)/shard_map/ppermute | solution.py:23
  108.9 1.9 collective-permute-done.3
  110.9 1.4 collective-permute-start.4
  112.3 1.3 collective-permute-start.5
  113.6 4.6 %collective-permute-done.5 = bf16[4,1,32,256]{3,2,1,0:T(8,128)(2,1)S(1)} collective-permute-done((bf16[4,1,32,256]{3,2,1,0:T(8,128)(2,1)S(1)}, bf16[4,1,32,256]{3,2,1,0:T(8,128)(2,1)S(1)}, u32[]{:S(2)}, u32[]{:S(2)}) %collective-permute-start.5) | collective-permute-done | bytes 65568 | tf_op jit(solution)/shard_map/ppermute | solution.py:34
  118.2 0.1 select_maximum_fusion
  118.7 0.3 convolution_bitcast_fusion
  119.0 0.3 convolution_bitcast_fusion.2
  119.4 0.3 convolution_bitcast_fusion.1
  119.7 2.0 pad_maximum_fusion
  121.8 47.5 %reduce-scatter.2.cloned.1.call-done = f32[864,128]{1,0:T(8,128)} async-done(((f32[6912,128]{1,0:T(8,128)}), f32[864,128]{1,0:T(8,128)}) %reduce-scatter.2.cloned.1.call-update) | async-done | bytes 442384 | tf_op jit(solution)/shard_map/reduce_scatter | solution.py:111
  169.3 38.1 %all-reduce.2 = (f32[256]{0:T(256)S(1)}, f32[256]{0:T(256)S(1)}) all-reduce(f32[256]{0:T(256)S(1)} %get-tuple-element.29, f32[256]{0:T(256)S(1)} %get-tuple-element.28), channel_id=1, replica_groups=mesh['tm'=4,'space'=8] {'tm','space'}, use_global_device_ids=true, to_apply=%region_10.11 | all-reduce | flops 512 | bytes 4096 | tf_op jit(solution)/shard_map/psum | solution.py:121
  207.4 0.1 reshape.151
  207.4 0.1 reduce_sum.84
  207.6 0.1 sub.41
  207.7 0.1 reshape.152
  207.8 0.1 reduce_sum.86
  208.0 0.1 mul.89
  208.1 0.7 fusion.32
  208.8 2.4 %reduce_sum.87 = f32[864,128]{1,0:T(8,128)} reduce(f32[4,864,128]{2,1,0:T(8,128)} %bitcast.59, f32[]{:T(128)} %constant.67.clone.1), dimensions={0}, to_apply=%region_13.14 | reduce | flops 331776 | bytes 2211844 | tf_op jit(solution)/shard_map/reduce_sum | solution.py:13
  (51 shorter events, 0.9 us)
Async XLA Ops:
  7.2 162.1 %reduce-scatter.2.cloned.1.call-start = ((), (), s32[]{:S(2)}) async-start(), calls=%async_computation.1 | async-start | bytes 3981312 | tf_op jit(solution)/shard_map/reduce_scatter | solution.py:111
  8.3 89.0 %collective-permute-start = (bf16[2,2,32,128]{3,2,1,0:T(8,128)(2,1)}, bf16[2,2,32,128]{3,2,1,0:T(8,128)(2,1)S(1)}, u32[]{:S(2)}, u32[]{:S(2)}) collective-permute-start(bf16[2,2,32,128]{3,2,1,0:T(8,128)(2,1)} %param.10), channel_id=1, source_target_pairs={{8,0},{16,8},{24,16},{9,1},{17,9},{25,17},{10,2},{18,10},{26,18},{... | collective-permute-start | bytes 98312 | tf_op jit(solution)/shard_map/ppermute | solution.py:23
  96.6 0.8 copy-start.1
  98.4 6.2 %copy-start = (bf16[2,2,32,256]{3,2,1,0:T(8,128)(2,1)S(1)}, bf16[2,2,32,256]{3,2,1,0:T(8,128)(2,1)}, u32[]{:S(2)}) copy-start(bf16[2,2,32,256]{3,2,1,0:T(8,128)(2,1)} %param.9) | copy-start | bytes 196612
  98.4 6.2 %copy-start.2 = (f32[256]{0:T(256)S(1)}, f32[256]{0:T(256)}, u32[]{:S(2)}) copy-start(f32[256]{0:T(256)} %param.12) | copy-start | bytes 3076
  98.4 6.2 %copy-start.3 = (f32[256]{0:T(256)S(1)}, f32[256]{0:T(256)}, u32[]{:S(2)}) copy-start(f32[256]{0:T(256)} %param.13) | copy-start | bytes 3076
  99.2 4.5 %collective-permute-start.1 = (f32[2,32,256]{2,1,0:T(8,128)S(1)}, f32[2,32,256]{2,1,0:T(8,128)S(1)}, u32[]{:S(2)}, u32[]{:S(2)}) collective-permute-start(f32[2,32,256]{2,1,0:T(8,128)S(1)} %get-tuple-element.54), channel_id=1, source_target_pairs={{1,0},{2,1},{3,2},{4,3},{5,4},{6,5},{7,6},{9,8},{10,9},{11,10},{12... | collective-permute-start | bytes 196616 | tf_op jit(solution)/shard_map/ppermute | solution.py:23
  100.6 3.9 %collective-permute-start.2 = (f32[2,32,256]{2,1,0:T(8,128)S(1)}, f32[2,32,256]{2,1,0:T(8,128)S(1)}, u32[]{:S(2)}, u32[]{:S(2)}) collective-permute-start(f32[2,32,256]{2,1,0:T(8,128)S(1)} %get-tuple-element.53), channel_id=1, source_target_pairs={{0,1},{1,2},{2,3},{3,4},{4,5},{5,6},{6,7},{8,9},{9,10},{10,11},{11... | collective-permute-start | bytes 196616 | tf_op jit(solution)/shard_map/ppermute | solution.py:23
  104.7 6.1 %collective-permute-start.3 = (bf16[2,2,32,256]{3,2,1,0:T(8,128)(2,1)S(1)}, bf16[2,2,32,256]{3,2,1,0:T(8,128)(2,1)S(1)}, u32[]{:S(2)}, u32[]{:S(2)}) collective-permute-start(bf16[2,2,32,256]{3,2,1,0:T(8,128)(2,1)S(1)} %get-tuple-element.90), channel_id=1, source_target_pairs={{0,8},{8,16},{16,24},{1,9},{9,17},{17,25},{2,10},{10,18},{18,26},{... | collective-permute-start | bytes 196616 | tf_op jit(solution)/shard_map/ppermute | solution.py:23
  110.9 2.8 %collective-permute-start.4 = (bf16[4,1,32,256]{3,2,1,0:T(8,128)(2,1)S(1)}, bf16[4,1,32,256]{3,2,1,0:T(8,128)(2,1)S(1)}, u32[]{:S(2)}, u32[]{:S(2)}) collective-permute-start(bf16[4,1,32,256]{3,2,1,0:T(8,128)(2,1)S(1)} %get-tuple-element.88), channel_id=1, source_target_pairs={{0,1},{1,2},{2,3},{3,4},{4,5},{5,6},{6,7},{8,9},{9,10},{10,11},{11... | collective-permute-start | bytes 196616 | tf_op jit(solution)/shard_map/ppermute | solution.py:31
  112.3 5.9 %collective-permute-start.5 = (bf16[4,1,32,256]{3,2,1,0:T(8,128)(2,1)S(1)}, bf16[4,1,32,256]{3,2,1,0:T(8,128)(2,1)S(1)}, u32[]{:S(2)}, u32[]{:S(2)}) collective-permute-start(bf16[4,1,32,256]{3,2,1,0:T(8,128)(2,1)S(1)} %get-tuple-element.89), channel_id=1, source_target_pairs={{1,0},{2,1},{3,2},{4,3},{5,4},{6,5},{7,6},{9,8},{10,9},{11,10},{12... | collective-permute-start | bytes 196616 | tf_op jit(solution)/shard_map/ppermute | solution.py:34
  121.7 87.1 %all-gather.3.cloned.1.call-start = ((), (), s32[]{:S(2)}) async-start(), calls=%async_computation.2 | async-start | bytes 2211840 | tf_op jit(solution)/shard_map/all_gather | solution.py:12
  207.3 3.8 %copy-start.4 = (f32[256]{0:T(256)}, f32[256]{0:T(256)S(1)}, u32[]{:S(2)}) copy-start(f32[256]{0:T(256)S(1)} %get-tuple-element.30) | copy-start | bytes 3076
  207.3 3.8 %copy-start.5 = (f32[256]{0:T(256)}, f32[256]{0:T(256)S(1)}, u32[]{:S(2)}) copy-start(f32[256]{0:T(256)S(1)} %get-tuple-element.31) | copy-start | bytes 3076
Sparse Core Ops, SparseCore 0:
  121.8 47.3 reduce-scatter.1
  171.2 31.3 all-gather.2
